TPU v7x, 256 devices: a whole 4x4x8 slice. The times are simulated.
256 devices in a mesh: ctx: 128 (over x, y, z_lo, core), head: 2 (over z_hi).
Axes of the slice: x: 4, y: 4, z: 8 (z_hi: 2, z_lo: 4; z = z_hi * 4 + z_lo), core: 2. Of those that a mesh axis runs over, the one named last changes fastest.
Arguments:
- latent: bfloat16 [16384, 512], P('ctx'), may hold values from -6 to 6
- rope_key: bfloat16 [16384, 64], P('ctx'), may hold values from -6 to 6
- queries: bfloat16 [16384, 64, 512], P('ctx', 'head'), may hold values from -89 to 89
- query_rope: bfloat16 [16384, 4096], P('ctx', 'head'), may hold values from -6 to 6
- grad_out: bfloat16 [16384, 64, 512], P('ctx', 'head'), may hold values from -6 to 6
- sel_blocks: int32 [256, 5], P('ctx'), may hold values from 0 to 255, as said below
Outputs:
- attention_out: bfloat16 [16384, 64, 512], P('ctx', 'head')
- d_latent: float32 [16384, 512], P('ctx')
- d_rope_key: float32 [16384, 64], P('ctx')
Inputs may be any that keep to these rules, and one draw needn't show every extreme that they name: `sel_blocks`: row b lists the key blocks of query block b: slot 0 holds b, slots 1 to min(b, 4) hold distinct blocks below b, any of them, and any later slots hold b and are not used.
All inputs are finite; a program needn't handle non-finite values.
Results may differ from a plain program's by a relative error of at most 0.007.
Values may be sent and summed in bfloat16 or wider, within the bound.
No kernel may reach another device: no remote copies, remote signals or barrier semaphores. Data moves between devices by JAX's collectives and lax.ppermute only.
A program may use at most 192 MiB of HBM per device.

v0:
```python
import jax
import jax.numpy as jnp
from jax import lax
from jax.sharding import PartitionSpec as P

BLK = 64
SEL = 5
softmax_scale = 192.0 ** (-0.5)
rope_base = 10000.0


def rotate_pairs(values, positions, direction):
    half_width = values.shape[-1] // 2
    freq_steps = jnp.arange(half_width, dtype=jnp.float32)
    inverse_freq = rope_base ** (-2.0 * freq_steps / values.shape[-1])
    angles = positions.astype(jnp.float32)[:, None] * inverse_freq[None, :]
    cosine = jnp.cos(angles)
    sine_part = jnp.sin(angles) * direction
    lower_half = values[:, :half_width]
    upper_half = values[:, half_width:]
    return jnp.concatenate(
        [
            lower_half * cosine - upper_half * sine_part,
            upper_half * cosine + lower_half * sine_part,
        ],
        axis=1,
    )


def shards(latent, rope_key, queries, query_rope, grad_out, sel_blocks):
    token_count = latent.shape[0]
    latent_width = latent.shape[1]
    rope_width = rope_key.shape[1]
    head_count = queries.shape[1]
    block_count = token_count // BLK
    ctx_position = lax.axis_index("ctx")
    positions = ctx_position * token_count + jnp.arange(token_count, dtype=jnp.int32)
    rotated = rotate_pairs(rope_key.astype(jnp.float32), positions, 1.0).astype(jnp.bfloat16)
    whole_latent, whole_rotated = (
        lax.all_gather(latent, "ctx", axis=0, tiled=True),
        lax.all_gather(rotated, "ctx", axis=0, tiled=True),
    )
    offsets = jnp.arange(BLK, dtype=jnp.int32)
    key_rows = (sel_blocks[:, :, None] * BLK + offsets[None, None, :]).reshape(
        block_count, SEL * BLK
    )
    latent_key_rows = whole_latent[key_rows]
    keys_rotated = whole_rotated[key_rows]
    joined_keys = jnp.concatenate([latent_key_rows, keys_rotated], axis=2)
    latent_query_rows = queries.reshape(block_count, BLK, head_count, latent_width)
    query_rotary = query_rope.reshape(block_count, BLK, head_count, rope_width)
    joined_queries = jnp.concatenate([latent_query_rows, query_rotary], axis=3)
    upstream_gradient = grad_out.reshape(block_count, BLK, head_count, latent_width)
    scores = jnp.einsum(
        "sicu,squ->sicq", joined_queries, joined_keys, preferred_element_type=jnp.float32
    )
    block_ids = ctx_position * block_count + jnp.arange(block_count, dtype=jnp.int32)
    slot_index = jnp.arange(SEL * BLK, dtype=jnp.int32) // BLK
    slot_valid = slot_index[None, :] < jnp.minimum(block_ids + 1, SEL)[:, None]
    query_pos = positions.reshape(block_count, BLK)
    allowed = slot_valid[:, None, :] & (key_rows[:, None, :] <= query_pos[:, :, None])
    scores = jnp.where(allowed[:, :, None, :], scores * softmax_scale, -jnp.inf)
    row_max = jnp.max(scores, axis=-1, keepdims=True)
    expon = jnp.exp(scores - row_max)
    probs = expon / jnp.sum(expon, axis=-1, keepdims=True)
    probability_lowered = probs.astype(jnp.bfloat16)
    attention_out = jnp.einsum(
        "gpac,gcs->gpas", probability_lowered, latent_key_rows, preferred_element_type=jnp.float32
    )
    attention_out = attention_out.astype(jnp.bfloat16).reshape(
        token_count, head_count, latent_width
    )
    dprobs = jnp.einsum(
        "sicu,squ->sicq", upstream_gradient, latent_key_rows, preferred_element_type=jnp.float32
    )
    row_delta = jnp.sum(probs * dprobs, axis=-1, keepdims=True)
    scores_gradient = (probs * (dprobs - row_delta)).astype(jnp.bfloat16)
    grad_latent = softmax_scale * jnp.einsum(
        "rcfg,rcfq->rgq", scores_gradient, latent_query_rows, preferred_element_type=jnp.float32
    )
    grad_latent = grad_latent + jnp.einsum(
        "rcfg,rcfq->rgq", probability_lowered, upstream_gradient, preferred_element_type=jnp.float32
    )
    grad_rotary = softmax_scale * jnp.einsum(
        "bthk,bthr->bkr", scores_gradient, query_rotary, preferred_element_type=jnp.float32
    )
    grad_terms = jnp.concatenate([grad_latent, grad_rotary], axis=2).reshape(
        block_count * SEL * BLK, latent_width + rope_width
    )
    flat_rows = key_rows.reshape(-1)
    local_rows = flat_rows
    local_rows = jnp.where(
        (local_rows >= 0) & (local_rows < token_count * lax.axis_size("ctx")),
        local_rows,
        token_count * lax.axis_size("ctx"),
    )
    empty = jnp.zeros((token_count * lax.axis_size("ctx"), latent_width + rope_width), jnp.float32)
    owned = lax.psum_scatter(
        empty.at[local_rows].add(grad_terms, mode="drop"), "ctx", scatter_dimension=0, tiled=True
    )
    owned = lax.psum(owned, "head")
    d_latent = owned[:, :latent_width]
    d_rope_key = rotate_pairs(owned[:, latent_width:], positions, -1.0)
    return (attention_out, d_latent, d_rope_key)


def solution(mesh):
    return jax.shard_map(
        shards,
        mesh=mesh,
        in_specs=(
            P("ctx", None),
            P("ctx", None),
            P("ctx", "head", None),
            P("ctx", "head"),
            P("ctx", "head", None),
            P("ctx", None),
        ),
        out_specs=(P("ctx", "head", None), P("ctx", None), P("ctx", None)),
        check_vma=False,
    )
```

profile of v0, /device:TPU:1, one launch (start us, length us, event | category | flops | bytes accessed | tf_op | source)
XLA Modules:
  0.0 1357.6 jit_solution(7002328799493679324)
XLA Ops:
  7.2 0.0 all-gather.5.cloned.1.call-start
  7.2 0.7 convert_element_type.21
  8.0 0.1 fusion.39
  8.1 0.6 pad_maximum_fusion.2
  8.7 0.0 all-gather.5.cloned.1.call-update
  8.8 0.0 all-gather.3.cloned.1.call-start
  8.8 0.7 all-gather.3.cloned.1.call-update
  9.5 0.0 reduce-scatter.2.cloned.1.call-start
  9.6 0.7 broadcast_multiply_fusion
  10.2 0.1 add.139
  10.3 0.1 add.147
  10.4 0.1 add.140
  10.5 0.1 add.142
  10.6 0.1 reshape.200
  10.6 0.1 iota_add_fusion
  10.7 0.1 add.156
  10.8 2.1 reshape.194
  12.9 0.1 broadcast_compare_fusion
  13.0 0.1 compare_and_fusion
  13.1 203.5 %all-gather.5.cloned.1.call-done = bf16[16384,64]{0,1:T(8,128)(2,1)} async-done(((bf16[128,64]{0,1:T(8,128)(2,1)}), bf16[16384,64]{0,1:T(8,128)(2,1)}) %all-gather.5.cloned.1.call-update) | async-done | bytes 2097168 | tf_op jit(solution)/shard_map/all_gather | solution.py:41
  216.7 4.7 copy.37
  221.4 4.4 gather_fusion.1
  225.9 206.5 %all-gather.3.cloned.1.call-done = bf16[16384,512]{1,0:T(8,128)(2,1)} async-done(((bf16[128,512]{1,0:T(8,128)(2,1)}), bf16[16384,512]{1,0:T(8,128)(2,1)}) %all-gather.3.cloned.1.call-update) | async-done | bytes 16777232 | tf_op jit(solution)/shard_map/all_gather | solution.py:40
  432.4 10.7 gather_fusion
  443.1 0.0 copy-start.1
  443.1 5.6 fusion.6
  448.7 0.0 copy-start.4
  448.7 23.1 %fusion.49 = (f32[2,64,32]{2,1,0:T(8,128)S(1)}, f32[2,64,32,320]{3,2,1,0:T(8,128)S(1)}) fusion(f32[2,64,32,320]{3,2,1,0:T(8,128)S(1)} %fusion.6, pred[2,64,320]{2,1,0:T(8,128)(4,1)S(1)} %compare_and_fusion), kind=kOutput, calls=%fused_computation.79 | output fusion | flops 7864639 | bytes 10543104 | tf_op jit(solution)/shard_map/sub | solution.py:64
  471.8 2.7 fusion.3
  474.6 0.0 copy-start.3
  474.6 1.7 fusion.5
  476.3 0.7 fusion.24
  477.0 1.6 fusion.20
  478.6 2.7 fusion.21
  481.3 0.1 copy.40
  481.5 0.1 pad_maximum_fusion
  481.6 23.6 %scatter_custom_fusion = f32[16384,576]{1,0:T(8,128)} fusion(s32[640]{0:T(1024)S(1)} %fusion.42, f32[640,576]{1,0:T(8,128)S(1)} %bitcast.49, f32[]{:T(128)} %constant.56.clone.1), kind=kCustom, calls=%fused_computation.4 | custom fusion | flops 368640 | bytes 37748740 | tf_op jit(solution)/shard_map/scatter-add | solution.py:99
  505.2 39.2 %copy.41 = f32[16384,576]{0,1:T(8,128)} copy(f32[16384,576]{1,0:T(8,128)} %scatter_custom_fusion) | data formatting | bytes 75497472 | tf_op jit(solution)/shard_map/scatter-add | solution.py:99
  544.4 0.0 reduce-scatter.2.cloned.1.call-update
  544.4 0.0 all-reduce.2.cloned.1.call-start
  544.4 753.9 %reduce-scatter.2.cloned.1.call-done = f32[128,576]{0,1:T(8,128)} async-done(((f32[16384,576]{0,1:T(8,128)}), f32[128,576]{0,1:T(8,128)}) %reduce-scatter.2.cloned.1.call-update) | async-done | bytes 294928 | tf_op jit(solution)/shard_map/reduce_scatter | solution.py:98
  1298.3 0.0 all-reduce.2.cloned.1.call-update
  1298.4 7.2 convolution_convert_fusion
  1305.6 42.2 %all-reduce.2.cloned.1.call-done = f32[128,576]{0,1:T(8,128)} async-done(((f32[128,576]{0,1:T(8,128)}), f32[128,576]{0,1:T(8,128)}) %all-reduce.2.cloned.1.call-update) | async-done | bytes 294928 | tf_op jit(solution)/shard_map/psum | solution.py:101
  1347.8 1.0 slice.29
  1348.8 0.8 copy.42
  1349.6 0.9 fusion.36
  1350.5 0.6 pad_maximum_fusion.1
  (17 shorter events, 0.1 us)
Async XLA Ops:
  7.2 209.5 %all-gather.5.cloned.1.call-start = ((), (), s32[]{:S(2)}) async-start(), calls=%async_computation.2 | async-start | bytes 2113536 | tf_op jit(solution)/shard_map/all_gather | solution.py:41
  8.8 423.6 %all-gather.3.cloned.1.call-start = ((), (), s32[]{:S(2)}) async-start(), calls=%async_computation.1 | async-start | bytes 16908288 | tf_op jit(solution)/shard_map/all_gather | solution.py:40
  9.5 1288.8 %reduce-scatter.2.cloned.1.call-start = ((), (), s32[]{:S(2)}) async-start(), calls=%async_computation.3 | async-start | bytes 38043648 | tf_op jit(solution)/shard_map/reduce_scatter | solution.py:98
  443.1 28.7 %copy-start.1 = (bf16[640,512]{1,0:T(8,128)(2,1)}, bf16[640,512]{1,0:T(8,128)(2,1)S(1)}, u32[]{:S(2)}) copy-start(bf16[640,512]{1,0:T(8,128)(2,1)S(1)} %gather_fusion) | copy-start | bytes 1966084
  448.7 23.1 %copy-start.4 = (bf16[128,32,512]{2,1,0:T(8,128)(2,1)S(1)}, bf16[128,32,512]{2,1,0:T(8,128)(2,1)}, u32[]{:S(2)}) copy-start(bf16[128,32,512]{2,1,0:T(8,128)(2,1)} %param.10) | copy-start | bytes 12582916
  471.8 6.8 copy-start
  474.6 2.4 copy-start.3
  544.4 754.0 %copy-start.2 = (bf16[640,512]{1,0:T(8,128)(2,1)S(1)}, bf16[640,512]{1,0:T(8,128)(2,1)}, u32[]{:S(2)}) copy-start(bf16[640,512]{1,0:T(8,128)(2,1)} %copy-done.1) | copy-start | bytes 1966084
  544.4 803.4 %all-reduce.2.cloned.1.call-start = ((), (), s32[]{:S(2)}) async-start(), calls=%async_computation.4 | async-start | bytes 589824 | tf_op jit(solution)/shard_map/psum | solution.py:101
Sparse Core Ops, SparseCore 0:
  10.4 206.2 all-gather.4
  218.5 213.7 all-gather.2
  544.5 753.7 reduce-scatter.1
  1300.8 46.9 all-reduce.1
where the time goes:
time: 1360 us
  waiting for transfers between devices  1210 us (89%)
  local copies, waits for them, and re-layouts  63.6 us (5%)
  other arithmetic  52.5 us (4%)
  matrix products  20.5 us (2%)
  between operations  14 us (1%)
    reduce_scatter x1, waiting for transfers between devices, shards(): lax.psum_scatter(empty.at[local_rows].add(grad_terms, mode='drop'), 'ctx'...  754 us
    all_gather x1, waiting for transfers between devices, shards(): lax.all_gather(latent, 'ctx', axis=0, tiled=True)  206 us
    all_gather x1, waiting for transfers between devices, shards(): lax.all_gather(rotated, 'ctx', axis=0, tiled=True)  204 us
    psum x1, waiting for transfers between devices, shards(): owned = lax.psum(owned, 'head')  42.2 us
    scatter-add x1, local copies, waits for them, and re-layouts, shards(): empty.at[local_rows].add(grad_terms, mode='drop')  39.2 us
  transfers between devices with their start and end apart: 4, of which 4 were waited for; matrix products, arithmetic and copies ran while one was open for 1% of the time, Pallas kernels for 0%

commit v1 on v0

--- a/solution.py
+++ b/solution.py
@@ -98,7 +98,7 @@
     owned = lax.psum_scatter(
         empty.at[local_rows].add(grad_terms, mode="drop"), "ctx", scatter_dimension=0, tiled=True
     )
-    owned = lax.psum(owned, "head")
+    owned = jnp.sum(lax.all_gather(owned, "head"), axis=0)
     d_latent = owned[:, :latent_width]
     d_rope_key = rotate_pairs(owned[:, latent_width:], positions, -1.0)
     return (attention_out, d_latent, d_rope_key)

time: 1360 us -> 1300 us (0.956)
  waiting for transfers between devices: 1210 us -> 1170 us
  local copies, waits for them, and re-layouts: 63.6 us -> 24.6 us
    psum x1 -> x0, waiting for transfers between devices: 42.2 us -> none  [shards(): owned = lax.psum(owned, 'head')]
    scatter-add x1 -> x0, local copies, waits for them, and re-layouts: 39.2 us -> none  [shards(): empty.at[local_rows].add(grad_terms, mode='drop')]
  transfers between devices with their start and end apart: 4 -> 3, of which waited for: 4 -> 3; matrix products, arithmetic and copies ran while one was open for 1% -> 2% of each run, Pallas kernels for 0% -> 0%
where the time goes in v1:
time: 1300 us; the launch traced here: 1290 us
  waiting for transfers between devices  1170 us (90%)
  other arithmetic  51.8 us (4%)
  local copies, waits for them, and re-layouts  24.6 us (2%)
  matrix products  20.5 us (2%)
  between operations  14 us (1%)
    reduce_scatter x1, waiting for transfers between devices, shards(): lax.psum_scatter(empty.at[local_rows].add(grad_terms, mode='drop'), 'ctx'...  759 us
    all_gather x1, waiting for transfers between devices, shards(): lax.all_gather(latent, 'ctx', axis=0, tiled=True)  206 us
    all_gather x1, waiting for transfers between devices, shards(): lax.all_gather(rotated, 'ctx', axis=0, tiled=True)  204 us
  transfers between devices with their start and end apart: 3, of which 3 were waited for; matrix products, arithmetic and copies ran while one was open for 2% of the time, Pallas kernels for 0%

profile of v1, /device:TPU:1, one launch (start us, length us, event | category | flops | bytes accessed | tf_op | source)
XLA Modules:
  0.0 1291.4 jit_solution(9620258601079557261)
XLA Ops:
  7.2 0.0 all-gather.6.cloned.1.call-start
  7.2 0.7 convert_element_type.21
  8.0 0.1 fusion.39
  8.1 0.6 pad_maximum_fusion.2
  8.7 0.0 all-gather.6.cloned.1.call-update
  8.8 0.0 all-gather.4.cloned.1.call-start
  8.8 0.7 all-gather.4.cloned.1.call-update
  9.5 0.0 reduce-scatter.2.cloned.1.call-start
  9.6 0.7 broadcast_multiply_fusion
  10.2 0.1 add.137
  10.3 0.1 add.145
  10.4 0.1 add.138
  10.5 0.1 add.140
  10.6 0.1 reshape.200
  10.6 0.1 iota_add_fusion
  10.7 0.1 add.154
  10.8 2.1 reshape.194
  12.9 0.1 broadcast_compare_fusion
  13.0 0.1 compare_and_fusion
  13.1 203.5 %all-gather.6.cloned.1.call-done = bf16[16384,64]{0,1:T(8,128)(2,1)} async-done(((bf16[128,64]{0,1:T(8,128)(2,1)}), bf16[16384,64]{0,1:T(8,128)(2,1)}) %all-gather.6.cloned.1.call-update) | async-done | bytes 2097168 | tf_op jit(solution)/shard_map/all_gather | solution.py:41
  216.7 4.7 copy.60
  221.4 4.4 gather_fusion.1
  225.9 206.5 %all-gather.4.cloned.1.call-done = bf16[16384,512]{1,0:T(8,128)(2,1)} async-done(((bf16[128,512]{1,0:T(8,128)(2,1)}), bf16[16384,512]{1,0:T(8,128)(2,1)}) %all-gather.4.cloned.1.call-update) | async-done | bytes 16777232 | tf_op jit(solution)/shard_map/all_gather | solution.py:40
  432.4 10.7 gather_fusion
  443.1 0.0 copy-start.1
  443.1 5.6 fusion.6
  448.7 0.0 copy-start.4
  448.7 23.1 %fusion.50 = (f32[2,64,32]{2,1,0:T(8,128)S(1)}, f32[2,64,32,320]{3,2,1,0:T(8,128)S(1)}) fusion(f32[2,64,32,320]{3,2,1,0:T(8,128)S(1)} %fusion.6, pred[2,64,320]{2,1,0:T(8,128)(4,1)S(1)} %compare_and_fusion), kind=kOutput, calls=%fused_computation.80 | output fusion | flops 7864639 | bytes 10543104 | tf_op jit(solution)/shard_map/sub | solution.py:64
  471.8 2.7 fusion.3
  474.6 0.0 copy-start.3
  474.6 1.7 fusion.5
  476.3 0.7 fusion.24
  477.0 1.6 fusion.20
  478.6 2.7 fusion.21
  481.3 0.1 copy.63
  481.5 0.1 pad_maximum_fusion
  481.6 23.6 %scatter_custom_fusion = f32[16384,576]{1,0:T(8,128)} fusion(s32[640]{0:T(1024)S(1)} %fusion.42, f32[640,576]{1,0:T(8,128)S(1)} %bitcast.51, f32[]{:T(128)} %constant.56.clone.1), kind=kCustom, calls=%fused_computation.4 | custom fusion | flops 368640 | bytes 37748740 | tf_op jit(solution)/shard_map/scatter-add | solution.py:99
  505.2 0.0 reduce-scatter.2.cloned.1.call-update
  505.2 1.1 copy-done.2
  506.3 7.2 convolution_convert_fusion
  513.5 758.9 %reduce-scatter.2.cloned.1.call-done = f32[128,576]{1,0:T(8,128)} async-done(((f32[16384,576]{1,0:T(8,128)}), f32[128,576]{1,0:T(8,128)}) %reduce-scatter.2.cloned.1.call-update) | async-done | bytes 294928 | tf_op jit(solution)/shard_map/reduce_scatter | solution.py:98
  1272.4 10.7 all-gather
  1283.1 0.1 fusion.49
  1283.2 0.7 slice.29
  1284.0 0.1 copy.76
  1284.0 0.1 copy.75
  1284.1 0.2 fusion.36
  1284.3 0.6 pad_maximum_fusion.1
  (17 shorter events, 0.1 us)
Async XLA Ops:
  7.2 209.5 %all-gather.6.cloned.1.call-start = ((), (), s32[]{:S(2)}) async-start(), calls=%async_computation.2 | async-start | bytes 2113536 | tf_op jit(solution)/shard_map/all_gather | solution.py:41
  8.8 423.6 %all-gather.4.cloned.1.call-start = ((), (), s32[]{:S(2)}) async-start(), calls=%async_computation.1 | async-start | bytes 16908288 | tf_op jit(solution)/shard_map/all_gather | solution.py:40
  9.5 1262.9 %reduce-scatter.2.cloned.1.call-start = ((), (), s32[]{:S(2)}) async-start(), calls=%async_computation.3 | async-start | bytes 42270720 | tf_op jit(solution)/shard_map/reduce_scatter | solution.py:98
  443.1 28.7 %copy-start.1 = (bf16[640,512]{1,0:T(8,128)(2,1)}, bf16[640,512]{1,0:T(8,128)(2,1)S(1)}, u32[]{:S(2)}) copy-start(bf16[640,512]{1,0:T(8,128)(2,1)S(1)} %gather_fusion) | copy-start | bytes 1966084
  448.7 23.1 %copy-start.4 = (bf16[128,32,512]{2,1,0:T(8,128)(2,1)S(1)}, bf16[128,32,512]{2,1,0:T(8,128)(2,1)}, u32[]{:S(2)}) copy-start(bf16[128,32,512]{2,1,0:T(8,128)(2,1)} %param.10) | copy-start | bytes 12582916
  471.8 6.8 copy-start
  474.6 2.4 copy-start.3
  505.2 1.1 copy-start.2
Sparse Core Ops, SparseCore 0:
  10.4 206.2 all-gather.5
  218.5 213.7 all-gather.3
  505.3 767.0 reduce-scatter.1
